TPU v7x, 32 devices: a whole 2x2x4 slice. The times are simulated.
32 devices in a mesh: dp: 8 (over z, y), rep: 4 (over x, core).
Axes of the slice: x: 2, y: 2, z: 4, core: 2. Of those that a mesh axis runs over, the one named last changes fastest.
Arguments:
- queries: bfloat16 [2048, 768], P(('dp', 'rep')), may hold values from -60 to 60
- bank: bfloat16 [64, 4096, 768], P('dp', 'rep'), may hold values from -0.21875 to 0.21875
- labels: int32 [64, 4096], P('dp', 'rep'), may hold values from 0 to 127
- probes: int32 [2048, 8], P(('dp', 'rep')), may hold values from 0 to 63, all different within a row; in each aligned block of 64 rows (0 to 63, 64 to 127, ...) at most 16 rows name the same one
Outputs:
- votes: float32 [2048, 128], P(('dp', 'rep'))
Inputs may be any that keep to these rules, and one draw needn't show every extreme that they name: `probes`: each row names 8 different clusters; among the rows of one device no cluster is named more than 16 times.
All inputs are finite; a program needn't handle non-finite values.
Results may differ from a plain program's by a relative error of at most 0.0017.
Values may be sent and summed in bfloat16 or wider, within the bound.
A program may use at most 192 MiB of HBM per device.

v0:
```python
import jax
import jax.numpy as jnp
from jax import lax
from jax.sharding import PartitionSpec as P

CLASSES = 128


logit_scale = 2.0


def partial_stats(arrived, bank_rows, label_rows):
    scores = logit_scale * jnp.einsum(
        "jcsd,cnd->jcsn", arrived, bank_rows, preferred_element_type=jnp.float32
    )
    highest = jnp.max(scores, axis=3)
    weights = jnp.exp(scores - highest[..., None])
    totals = jnp.sum(weights, axis=3)
    weights_half = weights.astype(jnp.bfloat16)
    one_hot = (label_rows[..., None] == lax.broadcasted_iota(jnp.int32, (1, 1, CLASSES), 2)).astype(
        jnp.bfloat16
    )
    tallies = jnp.einsum(
        "jcsn,cnk->jcsk", weights_half, one_hot, preferred_element_type=jnp.float32
    )
    return (highest, totals, tallies)


def fold_along(partials, along):
    top_value = jnp.max(partials[0], axis=along, keepdims=True)
    rescale = jnp.exp(partials[0] - top_value)
    return (
        jnp.squeeze(top_value, along),
        jnp.sum(partials[1] * rescale, axis=along),
        jnp.sum(partials[2] * rescale[..., None], axis=along),
    )


def local(queries, bank, labels, probes):
    query_count, feature_dim = queries.shape
    probe_count = probes.shape[1]
    local_clusters = bank.shape[0]
    home_count = lax.axis_size("dp")
    rep_count = lax.axis_size("rep")
    cluster_total = local_clusters * home_count
    slot_count = 2 * query_count * probe_count // cluster_total
    probe_flat = probes.reshape(-1)
    member = (probe_flat[:, None] == lax.broadcasted_iota(jnp.int32, (1, cluster_total), 1)).astype(
        jnp.int32
    )
    slot_rank = jnp.sum((jnp.cumsum(member, axis=0) - member) * member, axis=1)
    target_row = probe_flat * slot_count + slot_rank
    source_row = lax.broadcasted_iota(jnp.int32, (query_count * probe_count,), 0) // probe_count
    packed = (
        jnp.zeros((cluster_total * slot_count, feature_dim), jnp.bfloat16)
        .at[target_row]
        .set(queries[source_row])
    )
    arrived = lax.all_to_all(packed, "dp", split_axis=0, concat_axis=0, tiled=True)
    copies = lax.all_gather(arrived, "rep", axis=0, tiled=True)
    partials = partial_stats(
        copies.reshape(-1, local_clusters, slot_count, feature_dim), bank, labels
    )
    swapped = (
        lax.all_to_all(partials[0], "rep", split_axis=0, concat_axis=0, tiled=True),
        lax.all_to_all(partials[1], "rep", split_axis=0, concat_axis=0, tiled=True),
        lax.all_to_all(partials[2], "rep", split_axis=0, concat_axis=0, tiled=True),
    )
    grouped = tuple(
        (
            piece_array.reshape((rep_count, home_count) + piece_array.shape[1:])
            for piece_array in swapped
        )
    )
    merged = fold_along(grouped, 0)
    table = (
        lax.all_to_all(merged[0], "dp", split_axis=0, concat_axis=0, tiled=True),
        lax.all_to_all(merged[1], "dp", split_axis=0, concat_axis=0, tiled=True),
        lax.all_to_all(merged[2], "dp", split_axis=0, concat_axis=0, tiled=True),
    )
    highest = table[0].reshape(-1)[target_row].reshape(query_count, probe_count)
    totals = table[1].reshape(-1)[target_row].reshape(query_count, probe_count)
    tallies = table[2].reshape(-1, CLASSES)[target_row].reshape(query_count, probe_count, CLASSES)
    result = fold_along((highest, totals, tallies), 1)
    return CLASSES * result[2] / result[1][:, None]


def solution(mesh):
    return jax.shard_map(
        local,
        mesh=mesh,
        in_specs=(
            P(("dp", "rep"), None),
            P("dp", "rep", None),
            P("dp", "rep"),
            P(("dp", "rep"), None),
        ),
        out_specs=P(("dp", "rep"), None),
        check_vma=False,
    )
```

profile of v0, /device:TPU:0, one launch (start us, length us, event | category | flops | bytes accessed | tf_op | source)
XLA Modules:
  0.0 231.1 jit_solution(7498407559215826217)
XLA Ops:
  6.5 0.8 copy.47
  7.3 0.1 eq.45
  7.4 0.1 eq.41
  7.5 0.7 broadcast_multiply_fusion
  8.2 1.2 reduce-window.6
  9.5 0.2 slice_reduce_fusion
  9.7 0.1 copy.46
  9.8 0.1 mul.58
  9.9 0.1 fusion.23
  10.1 5.9 %scatter_custom_fusion = bf16[1024,768]{1,0:T(8,128)(2,1)S(1)} fusion(s32[512]{0:T(512)S(1)} %bitcast.66, bf16[64,768]{1,0:T(8,128)(2,1)S(1)} %copy-done, s32[1024]{0:T(1024)S(1)} %pad_clamp_fusion.1, bf16[]{:T(256)} %constant.14.clone.1), kind=kCustom, calls=%fused_computation.21 | custom fusion | bytes 1572866 | tf_op jit(solution)/shard_map/scatter | solution.py:57
  16.0 44.2 %all_to_all.42 = bf16[8,128,768]{2,1,0:T(8,128)(2,1)} all-to-all(bf16[8,128,768]{2,1,0:T(8,128)(2,1)S(1)} %bitcast.61), channel_id=1, replica_groups=mesh['dp'=8,'rep'=4] {'dp'}, dimensions={0} | all-to-all | bytes 3145728 | tf_op jit(solution)/shard_map/all_to_all | solution.py:59
  60.2 45.5 %all-gather.2.cloned.1.call-done = bf16[4096,768]{1,0:T(8,128)(2,1)} async-done(((bf16[1024,768]{1,0:T(8,128)(2,1)}), bf16[4096,768]{1,0:T(8,128)(2,1)}) %all-gather.2.cloned.1.call-update) | async-done | bytes 6291472 | tf_op jit(solution)/shard_map/all_gather | solution.py:60
  105.7 14.0 %bitcast_reduce_fusion = (f32[32,8,16]{2,0,1:T(8,128)S(1)}, f32[8,32,16,1024]{3,2,1,0:T(8,128)}) fusion(bf16[8,1024,768]{2,1,0:T(8,128)(2,1)} %param.5, bf16[32,8,16,768]{3,2,1,0:T(8,128)(2,1)} %bitcast.69), kind=kOutput, calls=%fused_computation.6 | convolution fusion | flops 6450835456 | bytes 35667968 | tf_op jit(solution)/shard_map/jcsd,cnd->jcsn/dot_general | solution.py:13
  119.7 10.3 %fusion.1 = (f32[32,8,16]{2,0,1:T(8,128)S(1)}, bf16[32,8,16,1024]{3,2,0,1:T(8,128)(2,1)}) fusion(f32[8,32,16,1024]{3,2,1,0:T(8,128)} %get-tuple-element.12, f32[32,8,16]{2,0,1:T(8,128)S(1)} %get-tuple-element.11), kind=kLoop, calls=%fused_computation.8 | loop fusion | flops 16773120 | bytes 25198592 | tf_op jit(solution)/shard_map/reduce_sum | solution.py:18
  130.1 0.7 reshape.216
  130.8 3.3 %all-to-all-start.5 = ((f32[4,1,1024]{2,1,0:T(1,128)}), f32[4,1,1024]{2,1,0:T(1,128)S(1)}, u32[]{:S(2)}, u32[]{:S(2)}) async-start(f32[4,1,1024]{2,1,0:T(1,128)} %reshape.216), calls=%async_computation.5 | async-start | bytes 32768 | tf_op jit(solution)/shard_map/all_to_all | solution.py:66
  134.2 0.7 reshape.212
  134.9 3.0 %all-to-all-done.5 = f32[4,1,1024]{2,1,0:T(1,128)S(1)} async-done(((f32[4,1,1024]{2,1,0:T(1,128)}), f32[4,1,1024]{2,1,0:T(1,128)S(1)}, u32[]{:S(2)}, u32[]{:S(2)}) %all-to-all-start.5) | async-done | bytes 16416 | tf_op jit(solution)/shard_map/all_to_all | solution.py:66
  137.9 3.2 %all-to-all-start.2 = ((f32[4,1,1024]{2,1,0:T(1,128)}), f32[4,1,1024]{2,1,0:T(1,128)S(1)}, u32[]{:S(2)}, u32[]{:S(2)}) async-start(f32[4,1,1024]{2,1,0:T(1,128)} %reshape.212), calls=%async_computation.2 | async-start | bytes 32768 | tf_op jit(solution)/shard_map/all_to_all | solution.py:65
  141.2 0.5 broadcast.146
  141.7 0.7 reduce.2
  142.3 0.1 reshape.217
  142.5 2.5 %all-to-all-done.2 = f32[4,1,1024]{2,1,0:T(1,128)S(1)} async-done(((f32[4,1,1024]{2,1,0:T(1,128)}), f32[4,1,1024]{2,1,0:T(1,128)S(1)}, u32[]{:S(2)}, u32[]{:S(2)}) %all-to-all-start.2) | async-done | bytes 16416 | tf_op jit(solution)/shard_map/all_to_all | solution.py:65
  145.0 0.7 reduce.3
  145.7 0.1 reshape.213
  145.9 0.7 reshape.218
  146.6 5.5 %all-to-all-start.6 = ((f32[8,1,128]{2,1,0:T(1,128)}), f32[8,1,128]{2,1,0:T(1,128)S(1)}, u32[]{:S(2)}, u32[]{:S(2)}) async-start(f32[8,1,128]{2,1,0:T(1,128)} %reshape.218), calls=%async_computation.6 | async-start | bytes 8192 | tf_op jit(solution)/shard_map/all_to_all | solution.py:78
  152.1 9.5 %fusion.12 = f32[32,8,16,128]{3,0,2,1:T(8,128)S(1)} fusion(bf16[32,8,16,1024]{3,2,0,1:T(8,128)(2,1)} %get-tuple-element.10, s32[8,1024]{1,0:T(8,128)S(1)} %copy-done.1), kind=kOutput, calls=%fused_computation.20 | convolution fusion | flops 1074790400 | bytes 10518528 | tf_op jit(solution)/shard_map/jcsn,cnk->jcsk/dot_general | solution.py:23
  161.6 2.6 %copy.52 = f32[32,8,16,128]{3,2,1,0:T(8,128)} copy(f32[32,8,16,128]{3,0,2,1:T(8,128)S(1)} %fusion.12) | data formatting | bytes 4194304 | tf_op jit(solution)/shard_map/jcsn,cnk->jcsk/transpose | solution.py:23
  164.2 3.6 %all-to-all-start.1 = ((f32[32,8,16,128]{3,2,1,0:T(8,128)}), f32[32,8,16,128]{3,2,1,0:T(8,128)S(1)}, u32[]{:S(2)}, u32[]{:S(2)}) async-start(f32[32,8,16,128]{3,2,1,0:T(8,128)} %copy.52), calls=%async_computation.1 | async-start | bytes 4194304 | tf_op jit(solution)/shard_map/all_to_all | solution.py:67
  167.8 0.7 reshape.214
  168.4 0.1 copy.56
  168.6 24.8 %all-to-all-done.1 = f32[32,8,16,128]{3,2,1,0:T(8,128)S(1)} async-done(((f32[32,8,16,128]{3,2,1,0:T(8,128)}), f32[32,8,16,128]{3,2,1,0:T(8,128)S(1)}, u32[]{:S(2)}, u32[]{:S(2)}) %all-to-all-start.1) | async-done | bytes 2097184 | tf_op jit(solution)/shard_map/all_to_all | solution.py:67
  193.4 6.0 %all-to-all-start.4 = ((f32[8,1,128]{2,1,0:T(1,128)}), f32[8,1,128]{2,1,0:T(1,128)S(1)}, u32[]{:S(2)}, u32[]{:S(2)}) async-start(f32[8,1,128]{2,1,0:T(1,128)} %reshape.214), calls=%async_computation.4 | async-start | bytes 8192 | tf_op jit(solution)/shard_map/all_to_all | solution.py:77
  199.4 1.6 fusion.10
  201.1 0.9 copy.58
  201.9 3.9 %all-to-all-done.4 = f32[8,1,128]{2,1,0:T(1,128)S(1)} async-done(((f32[8,1,128]{2,1,0:T(1,128)}), f32[8,1,128]{2,1,0:T(1,128)S(1)}, u32[]{:S(2)}, u32[]{:S(2)}) %all-to-all-start.4) | async-done | bytes 4128 | tf_op jit(solution)/shard_map/all_to_all | solution.py:77
  205.8 3.5 %all-to-all-start.3 = ((f32[8,8,16,128]{3,2,1,0:T(8,128)}), f32[8,8,16,128]{3,2,1,0:T(8,128)S(1)}, u32[]{:S(2)}, u32[]{:S(2)}) async-start(f32[8,8,16,128]{3,2,1,0:T(8,128)} %copy.58), calls=%async_computation.3 | async-start | bytes 1048576 | tf_op jit(solution)/shard_map/all_to_all | solution.py:79
  209.3 0.6 reduce.4
  210.1 2.3 gather_fusion.2
  212.5 0.6 reduce.5
  213.3 2.3 gather_fusion.1
  215.7 0.1 reduce_max.29
  215.8 0.2 multiply_reduce_fusion
  216.0 6.4 %all-to-all-done.3 = f32[8,8,16,128]{3,2,1,0:T(8,128)S(1)} async-done(((f32[8,8,16,128]{3,2,1,0:T(8,128)}), f32[8,8,16,128]{3,2,1,0:T(8,128)S(1)}, u32[]{:S(2)}, u32[]{:S(2)}) %all-to-all-start.3) | async-done | bytes 524320 | tf_op jit(solution)/shard_map/all_to_all | solution.py:79
  222.4 1.0 gather_fusion
  223.4 0.1 fusion.20
  223.6 0.7 multiply_divide_fusion
  (26 shorter events, 0.8 us)
Async XLA Ops:
  6.5 3.5 %copy-start = (bf16[64,768]{1,0:T(8,128)(2,1)S(1)}, bf16[64,768]{1,0:T(8,128)(2,1)}, u32[]{:S(2)}) copy-start(bf16[64,768]{1,0:T(8,128)(2,1)} %param.4) | copy-start | bytes 294916
  6.5 99.2 %all-gather.2.cloned.1.call-start = ((), (), s32[]{:S(2)}) async-start(), calls=%async_computation.7 | async-start | bytes 7864320 | tf_op jit(solution)/shard_map/all_gather | solution.py:60
  119.7 32.4 %copy-start.1 = (s32[8,1024]{1,0:T(8,128)S(1)}, s32[8,1024]{1,0:T(8,128)}, u32[]{:S(2)}) copy-start(s32[8,1024]{1,0:T(8,128)} %param.6) | copy-start | bytes 98308
  130.8 7.1 %all-to-all-start.5 = ((f32[4,1,1024]{2,1,0:T(1,128)}), f32[4,1,1024]{2,1,0:T(1,128)S(1)}, u32[]{:S(2)}, u32[]{:S(2)}) async-start(f32[4,1,1024]{2,1,0:T(1,128)} %reshape.216), calls=%async_computation.5 | async-start | bytes 32768 | tf_op jit(solution)/shard_map/all_to_all | solution.py:66
  137.9 7.1 %all-to-all-start.2 = ((f32[4,1,1024]{2,1,0:T(1,128)}), f32[4,1,1024]{2,1,0:T(1,128)S(1)}, u32[]{:S(2)}, u32[]{:S(2)}) async-start(f32[4,1,1024]{2,1,0:T(1,128)} %reshape.212), calls=%async_computation.2 | async-start | bytes 32768 | tf_op jit(solution)/shard_map/all_to_all | solution.py:65
  146.6 17.6 %all-to-all-start.6 = ((f32[8,1,128]{2,1,0:T(1,128)}), f32[8,1,128]{2,1,0:T(1,128)S(1)}, u32[]{:S(2)}, u32[]{:S(2)}) async-start(f32[8,1,128]{2,1,0:T(1,128)} %reshape.218), calls=%async_computation.6 | async-start | bytes 8192 | tf_op jit(solution)/shard_map/all_to_all | solution.py:78
  164.2 29.3 %all-to-all-start.1 = ((f32[32,8,16,128]{3,2,1,0:T(8,128)}), f32[32,8,16,128]{3,2,1,0:T(8,128)S(1)}, u32[]{:S(2)}, u32[]{:S(2)}) async-start(f32[32,8,16,128]{3,2,1,0:T(8,128)} %copy.52), calls=%async_computation.1 | async-start | bytes 4194304 | tf_op jit(solution)/shard_map/all_to_all | solution.py:67
  193.4 12.4 %all-to-all-start.4 = ((f32[8,1,128]{2,1,0:T(1,128)}), f32[8,1,128]{2,1,0:T(1,128)S(1)}, u32[]{:S(2)}, u32[]{:S(2)}) async-start(f32[8,1,128]{2,1,0:T(1,128)} %reshape.214), calls=%async_computation.4 | async-start | bytes 8192 | tf_op jit(solution)/shard_map/all_to_all | solution.py:77
  205.8 16.6 %all-to-all-start.3 = ((f32[8,8,16,128]{3,2,1,0:T(8,128)}), f32[8,8,16,128]{3,2,1,0:T(8,128)S(1)}, u32[]{:S(2)}, u32[]{:S(2)}) async-start(f32[8,8,16,128]{3,2,1,0:T(8,128)} %copy.58), calls=%async_computation.3 | async-start | bytes 1048576 | tf_op jit(solution)/shard_map/all_to_all | solution.py:79
Sparse Core Ops, SparseCore 0:
  60.3 45.3 all-gather.1
where the time goes:
time: 232 us; the launch traced here: 231 us
  waiting for transfers between devices  86.2 us (37%)
  blocking collectives  44.2 us (19%)
  starting transfers between devices  25.1 us (11%)
  matrix products  23.5 us (10%)
  local copies, waits for them, and re-layouts  20.7 us (9%)
  other arithmetic  17.8 us (8%)
  between operations  13.6 us (6%)
    all_gather x1, waiting for transfers between devices, local(): copies = lax.all_gather(arrived, 'rep', axis=0, tiled=True)  45.5 us
    all_to_all x1, blocking collectives, local(): lax.all_to_all(packed, 'dp', split_axis=0, concat_axis=0, tiled=True)  44.2 us
    all_to_all x1, waiting for transfers between devices, local(): lax.all_to_all(partials[2], 'rep', split_axis=0, concat_axis=0, tiled=True)  24.8 us
    dot_general x1, matrix products, partial_stats(): jnp.einsum('jcsd,cnd->jcsn', arrived, bank_rows, preferred_element_type=j...  14 us
    reduce_sum x1, other arithmetic, partial_stats(): totals = jnp.sum(weights, axis=3)  10.3 us
    dot_general x1, matrix products, partial_stats(): jnp.einsum('jcsn,cnk->jcsk', weights_half, one_hot, preferred_element_typ...  9.49 us
    all_to_all x1, waiting for transfers between devices, local(): lax.all_to_all(merged[2], 'dp', split_axis=0, concat_axis=0, tiled=True)  6.39 us
    all_to_all x1, starting transfers between devices, local(): lax.all_to_all(merged[0], 'dp', split_axis=0, concat_axis=0, tiled=True)  5.99 us
  transfers between devices with their start and end apart: 7, of which 6 were waited for; matrix products, arithmetic and copies ran while one was open for 10% of the time, Pallas kernels for 0%

commit v1 on v0

v1 whole, which is shorter than its diff:
```python
import functools

import jax
import jax.numpy as jnp
from jax import lax
from jax.experimental import pallas as pl
from jax.experimental.pallas import tpu as pltpu
from jax.sharding import PartitionSpec as P

CLASSES = 128
LANES = 128
LOGIT_SCALE = 2.0
LOW = -3.0e38
MESH = pl.DeviceIdType.MESH


def kernel(cfg, msg_ref, labels_ref, bank_ref, out_ref,
           bank_v, code, qs, s_buf, top_b, tot_b, tal, send_t, send_s,
           recv_t, recv_s, pair_out, pair_in, turned,
           bank_sem, st_sem, ss_sem, rt_sem, rs_sem, ps_sem, pr_sem):
    n_rep, n, q, cap, clusters, rows, depth, probe_count, group = cfg
    groups, width, span = n // group, group * q, group * cap
    pieces = depth // LANES
    me_dp, me_rep = lax.axis_index("dp"), lax.axis_index("rep")
    me = me_dp * n_rep + me_rep
    my_group, my_place = me // group, lax.rem(me, group)

    def device(flat):
        return (flat // n_rep, lax.rem(flat, n_rep))

    for c in range(clusters):
        pltpu.make_async_copy(bank_ref.at[c], bank_v.at[c], bank_sem.at[c]).start()

    barrier = pltpu.get_barrier_semaphore()

    def greet(flat):
        pl.semaphore_signal(barrier, inc=1, device_id=device(flat), device_id_type=MESH)

    for j in range(1, groups):
        greet(lax.rem(my_group + j, groups) * group + my_place)
    for j in range(1, group):
        greet(my_group * group + lax.rem(my_place + j, group))
    pl.semaphore_wait(barrier, groups + group - 2)

    lane = lax.broadcasted_iota(jnp.int32, (width, width), 1)
    row = lax.broadcasted_iota(jnp.int32, (width, width), 0)
    before = jnp.where((row < lane) & (row // q == lane // q), 1.0, 0.0).astype(jnp.bfloat16)
    offset = (lax.broadcasted_iota(jnp.int32, (1, width), 1) // q) * cap
    slot_iota = lax.broadcasted_iota(jnp.int32, (span, width), 0)
    first = me_dp * clusters

    def pick(g, _):
        named = msg_ref[g * group, pieces * q : pieces * q + 16, :].astype(jnp.float32)
        for j in range(1, group):
            named = jnp.maximum(
                named, msg_ref[g * group + j, pieces * q : pieces * q + 16, :].astype(jnp.float32))
        if width != LANES:
            named = jnp.concatenate(
                [msg_ref[g * group + j, pieces * q : pieces * q + 16, :].astype(jnp.float32)[:, :q]
                 for j in range(group)], axis=1)
        members = [
            jnp.max(jnp.where(named == (first + c).astype(jnp.float32), 1.0, 0.0), axis=0, keepdims=True)
            for c in range(clusters)
        ]
        member = jnp.concatenate(members, axis=0)
        rank = jnp.dot(member.astype(jnp.bfloat16), before, preferred_element_type=jnp.float32)
        place = jnp.where(member > 0.5, rank.astype(jnp.int32) + offset, -1)
        code[g] = place
        hot = jnp.concatenate(
            [jnp.where(slot_iota == place[c : c + 1, :], LOGIT_SCALE, 0.0) for c in range(clusters)], axis=0
        ).astype(jnp.bfloat16)
        block = jnp.concatenate(
            [
                jnp.concatenate(
                    [msg_ref[g * group + j, p * q : (p + 1) * q, :] for p in range(pieces)], axis=1)
                for j in range(group)
            ],
            axis=0,
        )
        picked = jnp.dot(hot, block, preferred_element_type=jnp.float32).astype(jnp.bfloat16)
        for c in range(clusters):
            qs[c, g] = picked[c * span : (c + 1) * span]
        return 0

    lax.fori_loop(0, groups, pick, 0)

    half = groups // 2
    slots = half * span
    class_iota = lax.broadcasted_iota(jnp.int32, (CLASSES, rows), 0)

    def score(c, h):
        picked = qs[c, h * half : (h + 1) * half].reshape(slots, depth)
        s_buf[h] = lax.dot_general(
            picked, bank_v[c], (((1,), (1,)), ((), ())), preferred_element_type=jnp.float32)

    def weigh(c, h):
        s = s_buf[h]
        top = jnp.max(s, axis=1, keepdims=True)
        e = jnp.exp(s - top)
        total = jnp.sum(e, axis=1, keepdims=True)
        hot = jnp.where(class_iota == labels_ref[pl.ds(c, 1), :], 1.0, 0.0).astype(jnp.bfloat16)
        tally = lax.dot_general(
            e.astype(jnp.bfloat16), hot, (((1,), (1,)), ((), ())), preferred_element_type=jnp.float32)
        where = slice(h * half, (h + 1) * half)
        top_b[c, where] = jnp.broadcast_to(top, (slots, LANES)).reshape(half, span, LANES)
        tot_b[c, where] = jnp.broadcast_to(total, (slots, LANES)).reshape(half, span, LANES)
        tal[c, where] = tally.reshape(half, span, CLASSES)

    def wait_bank(c):
        pltpu.make_async_copy(bank_ref.at[c], bank_v.at[c], bank_sem.at[c]).wait()

    wait_bank(0)
    score(0, 0)

    def cluster(c, _):
        score(c, 1)
        weigh(c, 0)

        @pl.when(c + 1 < clusters)
        def _():
            wait_bank(c + 1)

        score(jnp.minimum(c + 1, clusters - 1), 0)
        weigh(c, 1)
        return 0

    lax.fori_loop(0, clusters, cluster, 0)

    def copies(g):
        target = device(g * group + my_place)
        return (
            pltpu.make_async_remote_copy(
                src_ref=send_t.at[g], dst_ref=recv_t.at[my_group], send_sem=st_sem.at[g],
                recv_sem=rt_sem.at[my_group], device_id=target, device_id_type=MESH),
            pltpu.make_async_remote_copy(
                src_ref=send_s.at[g], dst_ref=recv_s.at[my_group], send_sem=ss_sem.at[g],
                recv_sem=rs_sem.at[my_group], device_id=target, device_id_type=MESH),
        )

    wide = max(1, width // LANES)

    def merge(j, _):
        g = lax.rem(my_group + j, groups)
        place = code[g]
        hots, tops = [], []
        for c in range(clusters):
            hot = slot_iota == place[c : c + 1, :]
            hots.append(hot)
            here = jnp.concatenate([top_b[c, g]] * wide, axis=1)
            tops.append(jnp.max(jnp.where(hot, here, LOW), axis=0, keepdims=True))
        highest = functools.reduce(jnp.maximum, tops)
        total = jnp.zeros((1, width), jnp.float32)
        scaled = []
        for c in range(clusters):
            w = jnp.exp(tops[c] - highest)
            here = jnp.concatenate([tot_b[c, g]] * wide, axis=1)
            total = total + w * jnp.sum(jnp.where(hots[c], here, 0.0), axis=0, keepdims=True)
            scaled.append(jnp.where(hots[c], w, 0.0))
        weight = jnp.concatenate(scaled, axis=0)
        tally = jnp.concatenate([tal[c, g] for c in range(clusters)], axis=0)
        w_hi = weight.astype(jnp.bfloat16)
        w_lo = (weight - w_hi.astype(jnp.float32)).astype(jnp.bfloat16)
        t_hi = tally.astype(jnp.bfloat16)
        t_lo = (tally - t_hi.astype(jnp.float32)).astype(jnp.bfloat16)

        def turn(a, b):
            return lax.dot_general(a, b, (((0,), (0,)), ((), ())), preferred_element_type=jnp.float32)

        merged = turn(t_hi, w_hi) + (turn(t_hi, w_lo) + turn(t_lo, w_hi))
        stats = jnp.concatenate([highest, total] + [jnp.zeros((1, width), jnp.float32)] * 6, axis=0)

        send_t[g] = merged.astype(jnp.bfloat16)
        send_s[g] = stats

        @pl.when(j < groups)
        def _():
            for copy in copies(g):
                copy.start()

        return 0

    lax.fori_loop(1, groups + 1, merge, 0)
    recv_t[my_group] = send_t[my_group]
    recv_s[my_group] = send_s[my_group]

    def arrived(j, _):
        g = lax.rem(my_group + groups - j, groups)
        pltpu.make_async_remote_copy(
            src_ref=send_t.at[g], dst_ref=recv_t.at[g], send_sem=st_sem.at[g],
            recv_sem=rt_sem.at[g], device_id=device(g * group + my_place), device_id_type=MESH).wait_recv()
        pltpu.make_async_remote_copy(
            src_ref=send_s.at[g], dst_ref=recv_s.at[g], send_sem=ss_sem.at[g],
            recv_sem=rs_sem.at[g], device_id=device(g * group + my_place), device_id_type=MESH).wait_recv()
        return 0

    lax.fori_loop(1, groups, arrived, 0)

    highest = functools.reduce(jnp.maximum, [recv_s[g, 0:1, :] for g in range(groups)])
    total = jnp.zeros((1, width), jnp.float32)
    merged = jnp.zeros((CLASSES, width), jnp.float32)
    for g in range(groups):
        w = jnp.exp(recv_s[g, 0:1, :] - highest)
        total = total + w * recv_s[g, 1:2, :]
        merged = merged + w * recv_t[g].astype(jnp.float32)
    pair_out[0:CLASSES, :] = merged
    pair_out[CLASSES : CLASSES + 8, :] = jnp.concatenate(
        [highest, total] + [jnp.zeros((1, width), jnp.float32)] * 6, axis=0)

    def pair(j):
        return pltpu.make_async_remote_copy(
            src_ref=pair_out, dst_ref=pair_in.at[j], send_sem=ps_sem.at[j], recv_sem=pr_sem.at[j],
            device_id=device(my_group * group + lax.rem(my_place + j, group)), device_id_type=MESH)

    for j in range(1, group):
        pair(j).start()
    for j in range(1, group):
        pair(j).wait_recv()
    tops = [highest] + [pair_in[j, CLASSES : CLASSES + 1, :] for j in range(1, group)]
    best = functools.reduce(jnp.maximum, tops)
    w = jnp.exp(highest - best)
    total, merged = total * w, merged * w
    for j in range(1, group):
        w = jnp.exp(tops[j] - best)
        total = total + w * pair_in[j, CLASSES + 1 : CLASSES + 2, :]
        merged = merged + w * pair_in[j, 0:CLASSES, :]
    turned[...] = (CLASSES * merged / total).T
    out_ref[...] = turned[pl.ds(pl.multiple_of(my_place * q, q), q), :]

    def sent(j, _):
        for copy in copies(lax.rem(my_group + j, groups)):
            copy.wait_send()
        return 0

    lax.fori_loop(1, groups, sent, 0)
    for j in range(1, group):
        pair(j).wait_send()


def local(queries, bank, labels, probes):
    q, depth = queries.shape
    probe_count = probes.shape[1]
    clusters, rows, _ = bank.shape
    n_dp, n_rep = lax.axis_size("dp"), lax.axis_size("rep")
    n = n_dp * n_rep
    cap = 2 * q * probe_count // (clusters * n_dp)
    group = max(LANES // q, 16 // cap)
    groups, width, span = n // group, group * q, group * cap
    pieces = depth // LANES

    place = lax.rem(lax.axis_index("rep"), group)
    named = jnp.full((16, LANES), -1, jnp.bfloat16)
    shift = place * q if width == LANES else 0
    named = lax.dynamic_update_slice(named, probes.T.astype(jnp.bfloat16), (0, shift))
    message = jnp.concatenate(
        [queries[:, p * LANES : (p + 1) * LANES] for p in range(pieces)] + [named], axis=0)
    messages = lax.all_gather(message, ("dp", "rep"), axis=0)

    cfg = (n_rep, n, q, cap, clusters, rows, depth, probe_count, group)
    vmem = pl.BlockSpec(memory_space=pltpu.VMEM)
    f32, bf16 = jnp.float32, jnp.bfloat16
    return pl.pallas_call(
        functools.partial(kernel, cfg),
        out_shape=jax.ShapeDtypeStruct((q, CLASSES), f32),
        in_specs=[vmem, vmem, pl.BlockSpec(memory_space=pl.ANY)],
        out_specs=vmem,
        scratch_shapes=[
            pltpu.VMEM((clusters, rows, depth), bf16),
            pltpu.VMEM((groups, clusters, width), jnp.int32),
            pltpu.VMEM((clusters, groups, span, depth), bf16),
            pltpu.VMEM((2, groups // 2 * span, rows), f32),
            pltpu.VMEM((clusters, groups, span, LANES), f32),
            pltpu.VMEM((clusters, groups, span, LANES), f32),
            pltpu.VMEM((clusters, groups, span, CLASSES), f32),
            pltpu.VMEM((groups, CLASSES, width), bf16),
            pltpu.VMEM((groups, 8, width), f32),
            pltpu.VMEM((groups, CLASSES, width), bf16),
            pltpu.VMEM((groups, 8, width), f32),
            pltpu.VMEM((CLASSES + 8, width), f32),
            pltpu.VMEM((group, CLASSES + 8, width), f32),
            pltpu.VMEM((width, CLASSES), f32),
            pltpu.SemaphoreType.DMA((clusters,)),
            pltpu.SemaphoreType.DMA((groups,)),
            pltpu.SemaphoreType.DMA((groups,)),
            pltpu.SemaphoreType.DMA((groups,)),
            pltpu.SemaphoreType.DMA((groups,)),
            pltpu.SemaphoreType.DMA((group,)),
            pltpu.SemaphoreType.DMA((group,)),
        ],
        compiler_params=pltpu.CompilerParams(
            collective_id=0, has_side_effects=True, vmem_limit_bytes=56 * 1024 * 1024),
    )(messages, labels, bank)


def solution(mesh):
    return jax.shard_map(
        local,
        mesh=mesh,
        in_specs=(
            P(("dp", "rep"), None),
            P("dp", "rep", None),
            P("dp", "rep"),
            P(("dp", "rep"), None),
        ),
        out_specs=P(("dp", "rep"), None),
        check_vma=False,
    )
```

time: 232 us -> 126 us (0.54)
  the two profiles are of different devices: /device:TPU:0 before, /device:TPU:15 now
where the time goes in v1:
time: 126 us; the launch traced here: 125 us
  waiting for transfers between devices  59.1 us (47%)
  Pallas kernels  45.2 us (36%)
  between operations  13.4 us (11%)
  local copies, waits for them, and re-layouts  6.83 us (5%)
    all_gather x1, waiting for transfers between devices, local(): messages = lax.all_gather(message, ('dp', 'rep'), axis=0)  59.1 us
    pallas_call x1, Pallas kernels, local(): pl.pallas_call(functools.partial(kernel, cfg), out_shape=jax.ShapeDtypeSt...  45.2 us
    unnamed x9, local copies, waits for them, and re-layouts  6.34 us
  transfers between devices with their start and end apart: 1, of which 1 were waited for; matrix products, arithmetic and copies ran while one was open for 0% of the time, Pallas kernels for 0%

profile of v1, /device:TPU:15, one launch (start us, length us, event | category | flops | bytes accessed | tf_op | source)
XLA Modules:
  0.0 125.3 jit_solution(9378282994748576477)
XLA Ops:
  6.5 0.0 all-gather.3.cloned.1.call-start
  6.5 0.7 convert_bitcast_fusion
  7.2 0.7 constant_dynamic-update-slice_fusion.6
  7.9 0.7 constant_dynamic-update-slice_fusion.5
  8.7 0.7 constant_dynamic-update-slice_fusion.4
  9.4 0.7 constant_dynamic-update-slice_fusion.3
  10.1 0.7 constant_dynamic-update-slice_fusion.2
  10.8 0.7 constant_dynamic-update-slice_fusion.1
  11.6 0.5 dynamic_update_slice.3
  12.1 0.0 copy-start
  12.1 0.6 copy-done
  12.7 0.0 all-gather.3.cloned.1.call-update
  12.7 59.1 %all-gather.3.cloned.1.call-done = bf16[12800,128]{1,0:T(8,128)(2,1)} async-done(((bf16[400,128]{1,0:T(8,128)(2,1)}), bf16[12800,128]{1,0:T(8,128)(2,1)}) %all-gather.3.cloned.1.call-update) | async-done | bytes 3276816 | tf_op jit(solution)/shard_map/all_gather | solution.py:256
  71.8 45.2 %shard_map.46 = f32[64,128]{1,0:T(8,128)} custom-call(bf16[32,400,128]{2,1,0:T(8,128)(2,1)} %bitcast.3, s32[8,1024]{1,0:T(8,128)} %labels_ref.1, bf16[8,1024,768]{2,1,0:T(8,128)(2,1)} %bank_ref.1), custom_call_target="tpu_custom_call" | custom-call | tf_op jit(solution)/shard_map/pallas_call | solution.py:261
  117.1 1.4 %copy.13 = f32[64,128]{1,0:T(8,128)} copy(f32[64,128]{1,0:T(8,128)} %shard_map.46) | data formatting | bytes 65536
  (2 shorter events, 0.0 us)
Async XLA Ops:
  6.5 65.3 %all-gather.3.cloned.1.call-start = ((), (), s32[]{:S(2)}) async-start(), calls=%async_computation | async-start | bytes 3379200 | tf_op jit(solution)/shard_map/all_gather | solution.py:256
  12.1 0.6 copy-start
Sparse Core Ops, SparseCore 0:
  12.8 58.9 all-gather.2

commit v2 on v1

--- a/solution.py
+++ b/solution.py
@@ -14,10 +14,10 @@
 MESH = pl.DeviceIdType.MESH
 
 
-def kernel(cfg, msg_ref, labels_ref, bank_ref, out_ref,
-           bank_v, code, qs, s_buf, top_b, tot_b, tal, send_t, send_s,
+def kernel(cfg, query_ref, probe_ref, labels_ref, bank_ref, out_ref,
+           msg_ref, bank_v, code, qs, s_buf, top_b, tot_b, tal, send_t, send_s,
            recv_t, recv_s, pair_out, pair_in, turned,
-           bank_sem, st_sem, ss_sem, rt_sem, rs_sem, ps_sem, pr_sem):
+           bank_sem, go_sem, come_sem, st_sem, ss_sem, rt_sem, rs_sem, ps_sem, pr_sem):
     n_rep, n, q, cap, clusters, rows, depth, probe_count, group = cfg
     groups, width, span = n // group, group * q, group * cap
     pieces = depth // LANES
@@ -41,6 +41,111 @@
     for j in range(1, group):
         greet(my_group * group + lax.rem(my_place + j, group))
     pl.semaphore_wait(barrier, groups + group - 2)
+
+    line, z, y = lax.axis_size("dp") // 2, me_dp // 2, lax.rem(me_dp, 2)
+    x, core = me_rep // 2, lax.rem(me_rep, 2)
+    height = pieces * q + 16
+    cut = height // 32 * 16
+    whole, upper, lower = (0, height), (0, cut), (cut, height - cut)
+
+    def at(z_, y_, x_, core_):
+        return (z_ * 2 + y_) * n_rep + x_ * 2 + core_
+
+    def move(block, part, kind, target):
+        return pltpu.make_async_remote_copy(
+            src_ref=msg_ref.at[block, pl.ds(*part)], dst_ref=msg_ref.at[block, pl.ds(*part)],
+            send_sem=go_sem.at[block, kind], recv_sem=come_sem.at[block, 1 if part == lower else 0],
+            device_id=device(target), device_id_type=MESH)
+
+    sibling, over_x, over_y = at(z, y, x, 1 - core), at(z, y, 1 - x, core), at(z, 1 - y, x, core)
+    started = []
+
+    def start(condition, block, part, kind, target):
+        def run():
+            move(block, part, kind, target).start()
+
+        pl.when(condition)(run)
+        started.append((condition, block, part, kind, target))
+
+    def wait_for(condition, block, part, source):
+        def run():
+            move(block, part, 0, source).wait_recv()
+
+        pl.when(condition)(run)
+
+    def fan_out(b, there):
+        block = at(b, y, x, core)
+        start(there, block, whole, 2, over_x)
+        start(there, block, whole, 3, over_y)
+        start(there, block, whole, 4, sibling)
+
+    def step_line(t):
+        for b, there, source, onward, kind in (
+            (z - t, z - t >= 0, z - 1, z + 1, 0),
+            (z + t, z + t < line, z + 1, z - 1, 1),
+        ):
+            block = at(b, y, x, core)
+            wait_for(there, block, whole, at(source, y, x, core))
+            start(there & (onward >= 0) & (onward < line), block, whole, kind, at(onward, y, x, core))
+            fan_out(b, there)
+
+    def both(t):
+        if t == 0:
+            return ((z, z >= 0),)
+        return ((z - t, z - t >= 0), (z + t, z + t < line))
+
+    def step_cross(t):
+        for b, there in both(t):
+            block = at(b, y, 1 - x, core)
+            wait_for(there, block, whole, over_x)
+            start(there, block, upper, 3, over_y)
+            start(there, block, whole, 4, sibling)
+            block = at(b, 1 - y, x, core)
+            wait_for(there, block, whole, over_y)
+            start(there, block, lower, 2, over_x)
+            start(there, block, whole, 4, sibling)
+
+    def step_corner(t):
+        for b, there in both(t):
+            block = at(b, 1 - y, 1 - x, core)
+            wait_for(there, block, upper, over_y)
+            start(there, block, upper, 3, sibling)
+            wait_for(there, block, lower, over_x)
+            start(there, block, lower, 4, sibling)
+
+    def step_sibling(t):
+        for b, there in both(t):
+            wait_for(there, at(b, y, x, 1 - core), whole, sibling)
+            wait_for(there, at(b, y, 1 - x, 1 - core), whole, sibling)
+            wait_for(there, at(b, 1 - y, x, 1 - core), whole, sibling)
+            wait_for(there, at(b, 1 - y, 1 - x, 1 - core), upper, sibling)
+            wait_for(there, at(b, 1 - y, 1 - x, 1 - core), lower, sibling)
+
+    for p in range(pieces):
+        msg_ref[me, p * q : (p + 1) * q, :] = query_ref[:, p * LANES : (p + 1) * LANES]
+    shift = my_place * q if width == LANES else 0
+    spread = lax.broadcasted_iota(jnp.int32, (q, LANES), 1) == (
+        lax.broadcasted_iota(jnp.int32, (q, LANES), 0) + shift)
+    raised = jnp.concatenate(
+        [(probe_ref[...] + 1).astype(jnp.float32), jnp.zeros((q, 16 - probe_count), jnp.float32)],
+        axis=1).astype(jnp.bfloat16)
+    named_here = lax.dot_general(
+        raised, jnp.where(spread, 1.0, 0.0).astype(jnp.bfloat16), (((0,), (0,)), ((), ())),
+        preferred_element_type=jnp.float32)
+    msg_ref[me, pieces * q : height, :] = (named_here - 1.0).astype(jnp.bfloat16)
+
+    start(z + 1 < line, me, whole, 0, at(z + 1, y, x, core))
+    start(z >= 1, me, whole, 1, at(z - 1, y, x, core))
+    fan_out(z, z >= 0)
+    for t in range(line + 2):
+        if 1 <= t < line:
+            step_line(t)
+        if 1 <= t <= line:
+            step_cross(t - 1)
+        if t >= 2:
+            step_corner(t - 2)
+    for t in range(line):
+        step_sibling(t)
 
     lane = lax.broadcasted_iota(jnp.int32, (width, width), 1)
     row = lax.broadcasted_iota(jnp.int32, (width, width), 0)
@@ -226,6 +331,12 @@
     turned[...] = (CLASSES * merged / total).T
     out_ref[...] = turned[pl.ds(pl.multiple_of(my_place * q, q), q), :]
 
+    for condition, block, part, kind, target in started:
+        def run(block=block, part=part, kind=kind, target=target):
+            move(block, part, kind, target).wait_send()
+
+        pl.when(condition)(run)
+
     def sent(j, _):
         for copy in copies(lax.rem(my_group + j, groups)):
             copy.wait_send()
@@ -247,23 +358,16 @@
     groups, width, span = n // group, group * q, group * cap
     pieces = depth // LANES
 
-    place = lax.rem(lax.axis_index("rep"), group)
-    named = jnp.full((16, LANES), -1, jnp.bfloat16)
-    shift = place * q if width == LANES else 0
-    named = lax.dynamic_update_slice(named, probes.T.astype(jnp.bfloat16), (0, shift))
-    message = jnp.concatenate(
-        [queries[:, p * LANES : (p + 1) * LANES] for p in range(pieces)] + [named], axis=0)
-    messages = lax.all_gather(message, ("dp", "rep"), axis=0)
-
     cfg = (n_rep, n, q, cap, clusters, rows, depth, probe_count, group)
     vmem = pl.BlockSpec(memory_space=pltpu.VMEM)
     f32, bf16 = jnp.float32, jnp.bfloat16
     return pl.pallas_call(
         functools.partial(kernel, cfg),
         out_shape=jax.ShapeDtypeStruct((q, CLASSES), f32),
-        in_specs=[vmem, vmem, pl.BlockSpec(memory_space=pl.ANY)],
+        in_specs=[vmem, vmem, vmem, pl.BlockSpec(memory_space=pl.ANY)],
         out_specs=vmem,
         scratch_shapes=[
+            pltpu.VMEM((n, pieces * q + 16, LANES), bf16),
             pltpu.VMEM((clusters, rows, depth), bf16),
             pltpu.VMEM((groups, clusters, width), jnp.int32),
             pltpu.VMEM((clusters, groups, span, depth), bf16),
@@ -279,6 +383,8 @@
             pltpu.VMEM((group, CLASSES + 8, width), f32),
             pltpu.VMEM((width, CLASSES), f32),
             pltpu.SemaphoreType.DMA((clusters,)),
+            pltpu.SemaphoreType.DMA((n, 5)),
+            pltpu.SemaphoreType.DMA((n, 2)),
             pltpu.SemaphoreType.DMA((groups,)),
             pltpu.SemaphoreType.DMA((groups,)),
             pltpu.SemaphoreType.DMA((groups,)),
@@ -288,7 +394,7 @@
         ],
         compiler_params=pltpu.CompilerParams(
             collective_id=0, has_side_effects=True, vmem_limit_bytes=56 * 1024 * 1024),
-    )(messages, labels, bank)
+    )(queries, probes, labels, bank)
 
 
 def solution(mesh):

time: 126 us -> 67.9 us (0.54)
  waiting for transfers between devices: 59.1 us -> 0 us
  Pallas kernels: 45.2 us -> 64.9 us
  between operations: 13.4 us -> 0.01 us
  local copies, waits for them, and re-layouts: 6.83 us -> 2.76 us
    all_gather x1 -> x0, waiting for transfers between devices: 59.1 us -> none  [local(): messages = lax.all_gather(message, ('dp', 'rep'), axis=0)]
    pallas_call x1, Pallas kernels: 45.2 us -> 64.9 us  [local(): pl.pallas_call(functools.partial(kernel, cfg), out_shape=jax.ShapeDtypeSt...]
    unnamed x9 -> x2, local copies, waits for them, and re-layouts: 6.34 us -> 2.76 us
  transfers between devices with their start and end apart: 1 -> 0, of which waited for: 1 -> 0; matrix products, arithmetic and copies ran while one was open for 0% -> 0% of each run, Pallas kernels for 0% -> 0%
where the time goes in v2:
time: 67.9 us; the launch traced here: 67.7 us
  Pallas kernels  64.9 us (96%)
  local copies, waits for them, and re-layouts  2.76 us (4%)
    pallas_call x1, Pallas kernels, local(): pl.pallas_call(functools.partial(kernel, cfg), out_shape=jax.ShapeDtypeSt...  64.9 us
    unnamed x2, local copies, waits for them, and re-layouts  2.76 us

profile of v2, /device:TPU:15, one launch (start us, length us, event | category | flops | bytes accessed | tf_op | source)
XLA Modules:
  0.0 67.7 jit_solution(5555083846334799810)
XLA Ops:
  0.0 1.4 %copy.5.probe_ref = s32[64,8]{1,0:T(8,128)} copy(s32[64,8]{0,1:T(8,128)} %param.7) | data formatting | bytes 4096 | tf_op args[3]
  1.4 64.9 %shard_map.46 = f32[64,128]{1,0:T(8,128)} custom-call(bf16[64,768]{1,0:T(8,128)(2,1)} %query_ref.1, s32[64,8]{1,0:T(8,128)} %copy.5.probe_ref, s32[8,1024]{1,0:T(8,128)} %labels_ref.1, bf16[8,1024,768]{2,1,0:T(8,128)(2,1)} %bank_ref.1), custom_call_target="tpu_custom_call" | custom-call | tf_op jit(solution)/shard_map/pallas_call | solution.py:364
  66.3 1.4 %copy.7 = f32[64,128]{1,0:T(8,128)} copy(f32[64,128]{1,0:T(8,128)} %shard_map.46) | data formatting | bytes 65536

commit v3 on v2

--- a/solution.py
+++ b/solution.py
@@ -58,20 +58,24 @@
             device_id=device(target), device_id_type=MESH)
 
     sibling, over_x, over_y = at(z, y, x, 1 - core), at(z, y, 1 - x, core), at(z, 1 - y, x, core)
-    started = []
+    ending = []
 
     def start(condition, block, part, kind, target):
         def run():
-            move(block, part, kind, target).start()
+            copy = move(block, part, kind, target)
+            if ending:
+                copy.wait_send()
+            else:
+                copy.start()
 
         pl.when(condition)(run)
-        started.append((condition, block, part, kind, target))
 
     def wait_for(condition, block, part, source):
         def run():
             move(block, part, 0, source).wait_recv()
 
-        pl.when(condition)(run)
+        if not ending:
+            pl.when(condition)(run)
 
     def fan_out(b, there):
         block = at(b, y, x, core)
@@ -89,13 +93,17 @@
             start(there & (onward >= 0) & (onward < line), block, whole, kind, at(onward, y, x, core))
             fan_out(b, there)
 
-    def both(t):
+    def both(t, near):
         if t == 0:
-            return ((z, z >= 0),)
-        return ((z - t, z - t >= 0), (z + t, z + t < line))
-
-    def step_cross(t):
-        for b, there in both(t):
+            return ((z, z >= 0),) if near else ()
+        spots = ((z - t, z - t >= 0), (z + t, z + t < line))
+        mine = z // (line // 2)
+        if near:
+            return tuple((b, there & (b // (line // 2) == mine)) for b, there in spots)
+        return tuple((b, there & (b // (line // 2) != mine)) for b, there in spots)
+
+    def step_cross(t, near):
+        for b, there in both(t, near):
             block = at(b, y, 1 - x, core)
             wait_for(there, block, whole, over_x)
             start(there, block, upper, 3, over_y)
@@ -105,16 +113,16 @@
             start(there, block, lower, 2, over_x)
             start(there, block, whole, 4, sibling)
 
-    def step_corner(t):
-        for b, there in both(t):
+    def step_corner(t, near):
+        for b, there in both(t, near):
             block = at(b, 1 - y, 1 - x, core)
             wait_for(there, block, upper, over_y)
             start(there, block, upper, 3, sibling)
             wait_for(there, block, lower, over_x)
             start(there, block, lower, 4, sibling)
 
-    def step_sibling(t):
-        for b, there in both(t):
+    def step_sibling(t, near):
+        for b, there in both(t, near):
             wait_for(there, at(b, y, x, 1 - core), whole, sibling)
             wait_for(there, at(b, y, 1 - x, 1 - core), whole, sibling)
             wait_for(there, at(b, 1 - y, x, 1 - core), whole, sibling)
@@ -127,25 +135,36 @@
     spread = lax.broadcasted_iota(jnp.int32, (q, LANES), 1) == (
         lax.broadcasted_iota(jnp.int32, (q, LANES), 0) + shift)
     raised = jnp.concatenate(
-        [(probe_ref[...] + 1).astype(jnp.float32), jnp.zeros((q, 16 - probe_count), jnp.float32)],
-        axis=1).astype(jnp.bfloat16)
-    named_here = lax.dot_general(
-        raised, jnp.where(spread, 1.0, 0.0).astype(jnp.bfloat16), (((0,), (0,)), ((), ())),
-        preferred_element_type=jnp.float32)
+        [(probe_ref[...] + 1).astype(jnp.float32), jnp.zeros((16 - probe_count, q), jnp.float32)],
+        axis=0).astype(jnp.bfloat16)
+    named_here = jnp.dot(
+        raised, jnp.where(spread, 1.0, 0.0).astype(jnp.bfloat16), preferred_element_type=jnp.float32)
     msg_ref[me, pieces * q : height, :] = (named_here - 1.0).astype(jnp.bfloat16)
 
-    start(z + 1 < line, me, whole, 0, at(z + 1, y, x, core))
-    start(z >= 1, me, whole, 1, at(z - 1, y, x, core))
-    fan_out(z, z >= 0)
-    for t in range(line + 2):
-        if 1 <= t < line:
+    def step_own():
+        start(z + 1 < line, me, whole, 0, at(z + 1, y, x, core))
+        start(z >= 1, me, whole, 1, at(z - 1, y, x, core))
+        fan_out(z, z >= 0)
+
+    step_own()
+    close = line // 2
+    for t in range(line):
+        if t >= 1:
             step_line(t)
-        if 1 <= t <= line:
-            step_cross(t - 1)
-        if t >= 2:
-            step_corner(t - 2)
-    for t in range(line):
-        step_sibling(t)
+        if t < close:
+            step_cross(t, True)
+        if 1 <= t <= close:
+            step_corner(t - 1, True)
+    for t in range(close):
+        step_sibling(t, True)
+
+    def serve_cross():
+        for t in range(1, line):
+            step_cross(t, False)
+
+    def serve_corner():
+        for t in range(1, line):
+            step_corner(t, False)
 
     lane = lax.broadcasted_iota(jnp.int32, (width, width), 1)
     row = lax.broadcasted_iota(jnp.int32, (width, width), 0)
@@ -154,7 +173,8 @@
     slot_iota = lax.broadcasted_iota(jnp.int32, (span, width), 0)
     first = me_dp * clusters
 
-    def pick(g, _):
+    def pick(i, base):
+        g = base + i
         named = msg_ref[g * group, pieces * q : pieces * q + 16, :].astype(jnp.float32)
         for j in range(1, group):
             named = jnp.maximum(
@@ -185,28 +205,26 @@
         picked = jnp.dot(hot, block, preferred_element_type=jnp.float32).astype(jnp.bfloat16)
         for c in range(clusters):
             qs[c, g] = picked[c * span : (c + 1) * span]
-        return 0
-
-    lax.fori_loop(0, groups, pick, 0)
+        return base
 
     half = groups // 2
     slots = half * span
     class_iota = lax.broadcasted_iota(jnp.int32, (CLASSES, rows), 0)
 
-    def score(c, h):
-        picked = qs[c, h * half : (h + 1) * half].reshape(slots, depth)
-        s_buf[h] = lax.dot_general(
+    def score(c, base, buffer):
+        picked = qs[c, pl.ds(base, half)].reshape(slots, depth)
+        s_buf[buffer] = lax.dot_general(
             picked, bank_v[c], (((1,), (1,)), ((), ())), preferred_element_type=jnp.float32)
 
-    def weigh(c, h):
-        s = s_buf[h]
+    def weigh(c, base, buffer):
+        s = s_buf[buffer]
         top = jnp.max(s, axis=1, keepdims=True)
         e = jnp.exp(s - top)
         total = jnp.sum(e, axis=1, keepdims=True)
         hot = jnp.where(class_iota == labels_ref[pl.ds(c, 1), :], 1.0, 0.0).astype(jnp.bfloat16)
         tally = lax.dot_general(
             e.astype(jnp.bfloat16), hot, (((1,), (1,)), ((), ())), preferred_element_type=jnp.float32)
-        where = slice(h * half, (h + 1) * half)
+        where = pl.ds(base, half)
         top_b[c, where] = jnp.broadcast_to(top, (slots, LANES)).reshape(half, span, LANES)
         tot_b[c, where] = jnp.broadcast_to(total, (slots, LANES)).reshape(half, span, LANES)
         tal[c, where] = tally.reshape(half, span, CLASSES)
@@ -214,22 +232,30 @@
     def wait_bank(c):
         pltpu.make_async_copy(bank_ref.at[c], bank_v.at[c], bank_sem.at[c]).wait()
 
-    wait_bank(0)
-    score(0, 0)
-
-    def cluster(c, _):
-        score(c, 1)
-        weigh(c, 0)
-
-        @pl.when(c + 1 < clusters)
-        def _():
-            wait_bank(c + 1)
-
-        score(jnp.minimum(c + 1, clusters - 1), 0)
-        weigh(c, 1)
-        return 0
-
-    lax.fori_loop(0, clusters, cluster, 0)
+    def phase(base, near):
+        if near:
+            wait_bank(0)
+        score(0, base, 0)
+
+        def cluster(i, _):
+            c = 2 * i
+            if near:
+                wait_bank(c + 1)
+                wait_bank(c + 2)
+                pl.when(c == clusters // 4)(serve_cross)
+                pl.when(c == clusters // 2)(serve_corner)
+            score(c + 1, base, 1)
+            weigh(c, base, 0)
+            score(c + 2, base, 0)
+            weigh(c + 1, base, 1)
+            return 0
+
+        lax.fori_loop(0, clusters // 2 - 1, cluster, 0)
+        if near:
+            wait_bank(clusters - 1)
+        score(clusters - 1, base, 1)
+        weigh(clusters - 2, base, 0)
+        weigh(clusters - 1, base, 1)
 
     def copies(g):
         target = device(g * group + my_place)
@@ -244,8 +270,8 @@
 
     wide = max(1, width // LANES)
 
-    def merge(j, _):
-        g = lax.rem(my_group + j, groups)
+    def merge(j, base):
+        g = base + lax.rem(my_group + j, half)
         place = code[g]
         hots, tops = [], []
         for c in range(clusters):
@@ -277,36 +303,52 @@
         send_t[g] = merged.astype(jnp.bfloat16)
         send_s[g] = stats
 
-        @pl.when(j < groups)
+        @pl.when(g != my_group)
         def _():
             for copy in copies(g):
                 copy.start()
 
-        return 0
-
-    lax.fori_loop(1, groups + 1, merge, 0)
-    recv_t[my_group] = send_t[my_group]
-    recv_s[my_group] = send_s[my_group]
-
-    def arrived(j, _):
-        g = lax.rem(my_group + groups - j, groups)
-        pltpu.make_async_remote_copy(
-            src_ref=send_t.at[g], dst_ref=recv_t.at[g], send_sem=st_sem.at[g],
-            recv_sem=rt_sem.at[g], device_id=device(g * group + my_place), device_id_type=MESH).wait_recv()
-        pltpu.make_async_remote_copy(
-            src_ref=send_s.at[g], dst_ref=recv_s.at[g], send_sem=ss_sem.at[g],
-            recv_sem=rs_sem.at[g], device_id=device(g * group + my_place), device_id_type=MESH).wait_recv()
-        return 0
-
-    lax.fori_loop(1, groups, arrived, 0)
-
-    highest = functools.reduce(jnp.maximum, [recv_s[g, 0:1, :] for g in range(groups)])
-    total = jnp.zeros((1, width), jnp.float32)
-    merged = jnp.zeros((CLASSES, width), jnp.float32)
-    for g in range(groups):
-        w = jnp.exp(recv_s[g, 0:1, :] - highest)
-        total = total + w * recv_s[g, 1:2, :]
-        merged = merged + w * recv_t[g].astype(jnp.float32)
+        return base
+
+    near_base = my_group // half * half
+    far_base = half - near_base
+    lax.fori_loop(0, half, pick, near_base)
+    phase(near_base, True)
+    lax.fori_loop(1, half + 1, merge, near_base)
+    for t in range(1, line):
+        step_sibling(t, False)
+    lax.fori_loop(0, half, pick, far_base)
+    phase(far_base, False)
+    lax.fori_loop(1, half + 1, merge, far_base)
+
+    def gathered(state, place):
+        highest, total, merged = state
+        stats, tally = place
+        best = jnp.maximum(highest, stats[0:1, :])
+        keep, w = jnp.exp(highest - best), jnp.exp(stats[0:1, :] - best)
+        return (best, total * keep + w * stats[1:2, :], merged * keep + w * tally.astype(jnp.float32))
+
+    def arrived(base):
+        def one(j, state):
+            g = base + lax.rem(my_group + 2 * half - j, half)
+            for copy in (
+                pltpu.make_async_remote_copy(
+                    src_ref=send_t.at[g], dst_ref=recv_t.at[g], send_sem=st_sem.at[g], recv_sem=rt_sem.at[g],
+                    device_id=device(g * group + my_place), device_id_type=MESH),
+                pltpu.make_async_remote_copy(
+                    src_ref=send_s.at[g], dst_ref=recv_s.at[g], send_sem=ss_sem.at[g], recv_sem=rs_sem.at[g],
+                    device_id=device(g * group + my_place), device_id_type=MESH),
+            ):
+                copy.wait_recv()
+            return gathered(state, (recv_s[g], recv_t[g]))
+
+        return one
+
+    own = send_s[my_group]
+    state = (own[0:1, :], own[1:2, :], send_t[my_group].astype(jnp.float32))
+    state = lax.fori_loop(1, half, arrived(near_base), state)
+    state = lax.fori_loop(1, half + 1, arrived(far_base), state)
+    highest, total, merged = state
     pair_out[0:CLASSES, :] = merged
     pair_out[CLASSES : CLASSES + 8, :] = jnp.concatenate(
         [highest, total] + [jnp.zeros((1, width), jnp.float32)] * 6, axis=0)
@@ -328,14 +370,17 @@
         w = jnp.exp(tops[j] - best)
         total = total + w * pair_in[j, CLASSES + 1 : CLASSES + 2, :]
         merged = merged + w * pair_in[j, 0:CLASSES, :]
-    turned[...] = (CLASSES * merged / total).T
+    turned[...] = (merged / total).T
     out_ref[...] = turned[pl.ds(pl.multiple_of(my_place * q, q), q), :]
 
-    for condition, block, part, kind, target in started:
-        def run(block=block, part=part, kind=kind, target=target):
-            move(block, part, kind, target).wait_send()
-
-        pl.when(condition)(run)
+    ending.append(True)
+    step_own()
+    for t in range(line):
+        if t >= 1:
+            step_line(t)
+        for near in (True, False):
+            step_cross(t, near)
+            step_corner(t, near)
 
     def sent(j, _):
         for copy in copies(lax.rem(my_group + j, groups)):
@@ -394,7 +439,7 @@
         ],
         compiler_params=pltpu.CompilerParams(
             collective_id=0, has_side_effects=True, vmem_limit_bytes=56 * 1024 * 1024),
-    )(queries, probes, labels, bank)
+    )(queries, probes.T, labels, bank) * CLASSES
 
 
 def solution(mesh):

time: 67.9 us -> 62.7 us (0.923)
  the two profiles are of different devices: /device:TPU:15 before, /device:TPU:0 now
where the time goes in v3:
time: 62.7 us; the launch traced here: 62.5 us
  Pallas kernels  61.1 us (97%)
  other arithmetic  1.38 us (2%)
    pallas_call x1, Pallas kernels, local(): pl.pallas_call(functools.partial(kernel, cfg), out_shape=jax.ShapeDtypeSt...  61.1 us
    mul x1, other arithmetic, local(): pl.pallas_call(functools.partial(kernel, cfg), out_shape=jax.ShapeDtypeSt...  1.38 us

profile of v3, /device:TPU:0, one launch (start us, length us, event | category | flops | bytes accessed | tf_op | source)
XLA Modules:
  0.0 62.5 jit_solution(14823848348196674444)
XLA Ops:
  0.0 61.1 %shard_map.46 = f32[64,128]{1,0:T(8,128)} custom-call(bf16[64,768]{1,0:T(8,128)(2,1)} %query_ref.1, s32[8,64]{1,0:T(8,128)} %bitcast.1, s32[8,1024]{1,0:T(8,128)} %labels_ref.1, bf16[8,1024,768]{2,1,0:T(8,128)(2,1)} %bank_ref.1), custom_call_target="tpu_custom_call" | custom-call | tf_op jit(solution)/shard_map/pallas_call | solution.py:409
  61.2 1.4 %broadcast_multiply_fusion = f32[64,128]{1,0:T(8,128)} fusion(f32[64,128]{1,0:T(8,128)} %shard_map.46), kind=kLoop, calls=%fused_computation | loop fusion | flops 8192 | bytes 65536 | tf_op jit(solution)/shard_map/mul | solution.py:409

commit v4 on v3

--- a/solution.py
+++ b/solution.py
@@ -172,42 +172,48 @@
     offset = (lax.broadcasted_iota(jnp.int32, (1, width), 1) // q) * cap
     slot_iota = lax.broadcasted_iota(jnp.int32, (span, width), 0)
     first = me_dp * clusters
-
-    def pick(i, base):
-        g = base + i
-        named = msg_ref[g * group, pieces * q : pieces * q + 16, :].astype(jnp.float32)
-        for j in range(1, group):
-            named = jnp.maximum(
-                named, msg_ref[g * group + j, pieces * q : pieces * q + 16, :].astype(jnp.float32))
-        if width != LANES:
-            named = jnp.concatenate(
-                [msg_ref[g * group + j, pieces * q : pieces * q + 16, :].astype(jnp.float32)[:, :q]
-                 for j in range(group)], axis=1)
-        members = [
+    probe_rows = 16
+    half = groups // 2
+    batch = 4 if half % 4 == 0 else 1
+
+    def members_of(g):
+        blocks = [msg_ref[g * group + j, pieces * q : pieces * q + probe_rows, :].astype(jnp.float32)
+                  for j in range(group)]
+        if width == LANES:
+            named = functools.reduce(jnp.maximum, blocks)
+        else:
+            named = jnp.concatenate([block[:, :q] for block in blocks], axis=1)
+        return [
             jnp.max(jnp.where(named == (first + c).astype(jnp.float32), 1.0, 0.0), axis=0, keepdims=True)
             for c in range(clusters)
         ]
-        member = jnp.concatenate(members, axis=0)
+
+    def pick(i, base):
+        gs = [base + i * batch + k for k in range(batch)]
+        member = jnp.concatenate([m for g in gs for m in members_of(g)], axis=0)
         rank = jnp.dot(member.astype(jnp.bfloat16), before, preferred_element_type=jnp.float32)
-        place = jnp.where(member > 0.5, rank.astype(jnp.int32) + offset, -1)
-        code[g] = place
-        hot = jnp.concatenate(
-            [jnp.where(slot_iota == place[c : c + 1, :], LOGIT_SCALE, 0.0) for c in range(clusters)], axis=0
-        ).astype(jnp.bfloat16)
-        block = jnp.concatenate(
-            [
-                jnp.concatenate(
-                    [msg_ref[g * group + j, p * q : (p + 1) * q, :] for p in range(pieces)], axis=1)
-                for j in range(group)
-            ],
-            axis=0,
-        )
-        picked = jnp.dot(hot, block, preferred_element_type=jnp.float32).astype(jnp.bfloat16)
-        for c in range(clusters):
-            qs[c, g] = picked[c * span : (c + 1) * span]
+        places = jnp.where(member > 0.5, rank.astype(jnp.int32) + offset, -1)
+        picks = []
+        for k, g in enumerate(gs):
+            place = places[k * clusters : (k + 1) * clusters]
+            hot = jnp.concatenate(
+                [jnp.where(slot_iota == place[c : c + 1, :], LOGIT_SCALE, 0.0) for c in range(clusters)],
+                axis=0).astype(jnp.bfloat16)
+            block = jnp.concatenate(
+                [
+                    jnp.concatenate(
+                        [msg_ref[g * group + j, p * q : (p + 1) * q, :] for p in range(pieces)], axis=1)
+                    for j in range(group)
+                ],
+                axis=0,
+            )
+            picks.append(jnp.dot(hot, block, preferred_element_type=jnp.float32).astype(jnp.bfloat16))
+        for k, g in enumerate(gs):
+            code[g] = places[k * clusters : (k + 1) * clusters]
+            for c in range(clusters):
+                qs[c, g] = picks[k][c * span : (c + 1) * span]
         return base
 
-    half = groups // 2
     slots = half * span
     class_iota = lax.broadcasted_iota(jnp.int32, (CLASSES, rows), 0)
 
@@ -270,8 +276,7 @@
 
     wide = max(1, width // LANES)
 
-    def merge(j, base):
-        g = base + lax.rem(my_group + j, half)
+    def merged_of(g):
         place = code[g]
         hots, tops = [], []
         for c in range(clusters):
@@ -299,27 +304,33 @@
 
         merged = turn(t_hi, w_hi) + (turn(t_hi, w_lo) + turn(t_lo, w_hi))
         stats = jnp.concatenate([highest, total] + [jnp.zeros((1, width), jnp.float32)] * 6, axis=0)
-
-        send_t[g] = merged.astype(jnp.bfloat16)
-        send_s[g] = stats
-
-        @pl.when(g != my_group)
-        def _():
-            for copy in copies(g):
-                copy.start()
+        return merged.astype(jnp.bfloat16), stats
+
+    def merge(i, base):
+        gs = [base + lax.rem(my_group + 1 + i * batch + k, half) for k in range(batch)]
+        done = [merged_of(g) for g in gs]
+        for g, (merged, stats) in zip(gs, done):
+            send_t[g] = merged
+            send_s[g] = stats
+        for g in gs:
+
+            @pl.when(g != my_group)
+            def _(g=g):
+                for copy in copies(g):
+                    copy.start()
 
         return base
 
     near_base = my_group // half * half
     far_base = half - near_base
-    lax.fori_loop(0, half, pick, near_base)
+    lax.fori_loop(0, half // batch, pick, near_base)
     phase(near_base, True)
-    lax.fori_loop(1, half + 1, merge, near_base)
+    lax.fori_loop(0, half // batch, merge, near_base)
     for t in range(1, line):
         step_sibling(t, False)
-    lax.fori_loop(0, half, pick, far_base)
+    lax.fori_loop(0, half // batch, pick, far_base)
     phase(far_base, False)
-    lax.fori_loop(1, half + 1, merge, far_base)
+    lax.fori_loop(0, half // batch, merge, far_base)
 
     def gathered(state, place):
         highest, total, merged = state

time: 62.7 us -> 58.8 us (0.938)
  Pallas kernels: 61.1 us -> 57.2 us
    pallas_call x1, Pallas kernels: 61.1 us -> 57.2 us  [local(): pl.pallas_call(functools.partial(kernel, cfg), out_shape=jax.ShapeDtypeSt...]
where the time goes in v4:
time: 58.8 us; the launch traced here: 58.5 us
  Pallas kernels  57.2 us (97%)
  other arithmetic  1.38 us (2%)
    pallas_call x1, Pallas kernels, local(): pl.pallas_call(functools.partial(kernel, cfg), out_shape=jax.ShapeDtypeSt...  57.2 us
    mul x1, other arithmetic, local(): pl.pallas_call(functools.partial(kernel, cfg), out_shape=jax.ShapeDtypeSt...  1.38 us

profile of v4, /device:TPU:0, one launch (start us, length us, event | category | flops | bytes accessed | tf_op | source)
XLA Modules:
  0.0 58.5 jit_solution(14115509336297919080)
XLA Ops:
  0.0 57.2 %shard_map.46 = f32[64,128]{1,0:T(8,128)} custom-call(bf16[64,768]{1,0:T(8,128)(2,1)} %query_ref.1, s32[8,64]{1,0:T(8,128)} %bitcast.1, s32[8,1024]{1,0:T(8,128)} %labels_ref.1, bf16[8,1024,768]{2,1,0:T(8,128)(2,1)} %bank_ref.1), custom_call_target="tpu_custom_call" | custom-call | tf_op jit(solution)/shard_map/pallas_call | solution.py:420
  57.2 1.4 %broadcast_multiply_fusion = f32[64,128]{1,0:T(8,128)} fusion(f32[64,128]{1,0:T(8,128)} %shard_map.46), kind=kLoop, calls=%fused_computation | loop fusion | flops 8192 | bytes 65536 | tf_op jit(solution)/shard_map/mul | solution.py:420

commit v5 on v4

--- a/solution.py
+++ b/solution.py
@@ -220,20 +220,19 @@
     def score(c, base, buffer):
         picked = qs[c, pl.ds(base, half)].reshape(slots, depth)
         s_buf[buffer] = lax.dot_general(
-            picked, bank_v[c], (((1,), (1,)), ((), ())), preferred_element_type=jnp.float32)
+            bank_v[c], picked, (((1,), (1,)), ((), ())), preferred_element_type=jnp.float32)
 
     def weigh(c, base, buffer):
         s = s_buf[buffer]
-        top = jnp.max(s, axis=1, keepdims=True)
+        top = jnp.max(s, axis=0, keepdims=True)
         e = jnp.exp(s - top)
-        total = jnp.sum(e, axis=1, keepdims=True)
+        total = jnp.sum(e, axis=0, keepdims=True)
         hot = jnp.where(class_iota == labels_ref[pl.ds(c, 1), :], 1.0, 0.0).astype(jnp.bfloat16)
-        tally = lax.dot_general(
-            e.astype(jnp.bfloat16), hot, (((1,), (1,)), ((), ())), preferred_element_type=jnp.float32)
+        tally = jnp.dot(hot, e.astype(jnp.bfloat16), preferred_element_type=jnp.float32)
         where = pl.ds(base, half)
-        top_b[c, where] = jnp.broadcast_to(top, (slots, LANES)).reshape(half, span, LANES)
-        tot_b[c, where] = jnp.broadcast_to(total, (slots, LANES)).reshape(half, span, LANES)
-        tal[c, where] = tally.reshape(half, span, CLASSES)
+        top_b[c, where] = jnp.broadcast_to(top, (LANES, slots)).T.reshape(half, span, LANES)
+        tot_b[c, where] = jnp.broadcast_to(total, (LANES, slots)).T.reshape(half, span, LANES)
+        tal[c, where] = tally.T.reshape(half, span, CLASSES)
 
     def wait_bank(c):
         pltpu.make_async_copy(bank_ref.at[c], bank_v.at[c], bank_sem.at[c]).wait()
@@ -427,7 +426,7 @@
             pltpu.VMEM((clusters, rows, depth), bf16),
             pltpu.VMEM((groups, clusters, width), jnp.int32),
             pltpu.VMEM((clusters, groups, span, depth), bf16),
-            pltpu.VMEM((2, groups // 2 * span, rows), f32),
+            pltpu.VMEM((2, rows, groups // 2 * span), f32),
             pltpu.VMEM((clusters, groups, span, LANES), f32),
             pltpu.VMEM((clusters, groups, span, LANES), f32),
             pltpu.VMEM((clusters, groups, span, CLASSES), f32),

time: 58.8 us -> 59.3 us (level)
  no operation moved by 1% of the time
where the time goes in v5:
time: 59.3 us; the launch traced here: 59.1 us
  Pallas kernels  57.7 us (97%)
  other arithmetic  1.38 us (2%)
    pallas_call x1, Pallas kernels, local(): pl.pallas_call(functools.partial(kernel, cfg), out_shape=jax.ShapeDtypeSt...  57.7 us
    mul x1, other arithmetic, local(): pl.pallas_call(functools.partial(kernel, cfg), out_shape=jax.ShapeDtypeSt...  1.38 us

profile of v5, /device:TPU:0, one launch (start us, length us, event | category | flops | bytes accessed | tf_op | source)
XLA Modules:
  0.0 59.1 jit_solution(8255517269899701895)
XLA Ops:
  0.0 57.7 %shard_map.46 = f32[64,128]{1,0:T(8,128)} custom-call(bf16[64,768]{1,0:T(8,128)(2,1)} %query_ref.1, s32[8,64]{1,0:T(8,128)} %bitcast.1, s32[8,1024]{1,0:T(8,128)} %labels_ref.1, bf16[8,1024,768]{2,1,0:T(8,128)(2,1)} %bank_ref.1), custom_call_target="tpu_custom_call" | custom-call | tf_op jit(solution)/shard_map/pallas_call | solution.py:419
  57.7 1.4 %broadcast_multiply_fusion = f32[64,128]{1,0:T(8,128)} fusion(f32[64,128]{1,0:T(8,128)} %shard_map.46), kind=kLoop, calls=%fused_computation | loop fusion | flops 8192 | bytes 65536 | tf_op jit(solution)/shard_map/mul | solution.py:419

commit v6 on v4

--- a/solution.py
+++ b/solution.py
@@ -15,9 +15,9 @@
 
 
 def kernel(cfg, query_ref, probe_ref, labels_ref, bank_ref, out_ref,
-           msg_ref, bank_v, code, qs, s_buf, top_b, tot_b, tal, send_t, send_s,
+           msg_ref, bank_v, code, qs, s_buf, top_b, tot_b, tal, send_t, send_s, give, keep, take,
            recv_t, recv_s, pair_out, pair_in, turned,
-           bank_sem, go_sem, come_sem, st_sem, ss_sem, rt_sem, rs_sem, ps_sem, pr_sem):
+           bank_sem, go_sem, come_sem, st_sem, ss_sem, rt_sem, rs_sem, gs_sem, gr_sem, ps_sem, pr_sem):
     n_rep, n, q, cap, clusters, rows, depth, probe_count, group = cfg
     groups, width, span = n // group, group * q, group * cap
     pieces = depth // LANES
@@ -248,8 +248,8 @@
             if near:
                 wait_bank(c + 1)
                 wait_bank(c + 2)
-                pl.when(c == clusters // 4)(serve_cross)
-                pl.when(c == clusters // 2)(serve_corner)
+                pl.when(c == 0)(serve_cross)
+                pl.when(c == clusters // 4)(serve_corner)
             score(c + 1, base, 1)
             weigh(c, base, 0)
             score(c + 2, base, 0)
@@ -304,13 +304,13 @@
 
         merged = turn(t_hi, w_hi) + (turn(t_hi, w_lo) + turn(t_lo, w_hi))
         stats = jnp.concatenate([highest, total] + [jnp.zeros((1, width), jnp.float32)] * 6, axis=0)
-        return merged.astype(jnp.bfloat16), stats
+        return merged, stats
 
     def merge(i, base):
         gs = [base + lax.rem(my_group + 1 + i * batch + k, half) for k in range(batch)]
         done = [merged_of(g) for g in gs]
         for g, (merged, stats) in zip(gs, done):
-            send_t[g] = merged
+            send_t[g] = merged.astype(jnp.bfloat16)
             send_s[g] = stats
         for g in gs:
 
@@ -319,6 +319,46 @@
                 for copy in copies(g):
                     copy.start()
 
+        return base
+
+    def hand_over(k):
+        return pltpu.make_async_remote_copy(
+            src_ref=give.at[k], dst_ref=take.at[k], send_sem=gs_sem.at[k], recv_sem=gr_sem.at[k],
+            device_id=device(sibling), device_id_type=MESH)
+
+    shared = half // 2
+    chunk = 4 if shared % 4 == 0 else 1
+
+    def merge_shared(i, base, buffer, parity):
+        ks = [i * chunk + k for k in range(chunk)]
+        done = [merged_of(base + 2 * k + parity) for k in ks]
+        for k, (merged, stats) in zip(ks, done):
+            buffer[k, 0:CLASSES, :] = merged
+            buffer[k, CLASSES : CLASSES + 8, :] = stats
+
+    def merge_give(i, base):
+        merge_shared(i, base, give, 1 - core)
+        for k in range(chunk):
+            hand_over(i * chunk + k).start()
+        return base
+
+    def merge_keep(i, base):
+        merge_shared(i, base, keep, core)
+        return base
+
+    def merge_both(i, base):
+        k = lax.rem(my_group + i, shared)
+        g = base + 2 * k + core
+        hand_over(k).wait_recv()
+        mine, theirs = keep[k], take[k]
+        top_m, top_t = mine[CLASSES : CLASSES + 1], theirs[CLASSES : CLASSES + 1]
+        best = jnp.maximum(top_m, top_t)
+        w_m, w_t = jnp.exp(top_m - best), jnp.exp(top_t - best)
+        send_t[g] = (mine[0:CLASSES] * w_m + theirs[0:CLASSES] * w_t).astype(jnp.bfloat16)
+        total = mine[CLASSES + 1 : CLASSES + 2] * w_m + theirs[CLASSES + 1 : CLASSES + 2] * w_t
+        send_s[g] = jnp.concatenate([best, total] + [jnp.zeros((1, width), jnp.float32)] * 6, axis=0)
+        for copy in copies(g):
+            copy.start()
         return base
 
     near_base = my_group // half * half
@@ -330,7 +370,9 @@
         step_sibling(t, False)
     lax.fori_loop(0, half // batch, pick, far_base)
     phase(far_base, False)
-    lax.fori_loop(0, half // batch, merge, far_base)
+    lax.fori_loop(0, shared // chunk, merge_give, far_base)
+    lax.fori_loop(0, shared // chunk, merge_keep, far_base)
+    lax.fori_loop(0, shared, merge_both, far_base)
 
     def gathered(state, place):
         highest, total, merged = state
@@ -358,7 +400,8 @@
     own = send_s[my_group]
     state = (own[0:1, :], own[1:2, :], send_t[my_group].astype(jnp.float32))
     state = lax.fori_loop(1, half, arrived(near_base), state)
-    state = lax.fori_loop(1, half + 1, arrived(far_base), state)
+    served = lax.rem(lax.rem(my_group, half), 2) == core
+    state = lax.fori_loop(1, 1 + jnp.where(served, half, 0), arrived(far_base), state)
     highest, total, merged = state
     pair_out[0:CLASSES, :] = merged
     pair_out[CLASSES : CLASSES + 8, :] = jnp.concatenate(
@@ -393,12 +436,19 @@
             step_cross(t, near)
             step_corner(t, near)
 
-    def sent(j, _):
-        for copy in copies(lax.rem(my_group + j, groups)):
+    def sent_near(j, base):
+        for copy in copies(base + lax.rem(my_group + j, half)):
             copy.wait_send()
-        return 0
-
-    lax.fori_loop(1, groups, sent, 0)
+        return base
+
+    def sent_far(k, base):
+        hand_over(k).wait_send()
+        for copy in copies(base + 2 * k + core):
+            copy.wait_send()
+        return base
+
+    lax.fori_loop(1, half, sent_near, near_base)
+    lax.fori_loop(0, shared, sent_far, far_base)
     for j in range(1, group):
         pair(j).wait_send()
 
@@ -433,6 +483,9 @@
             pltpu.VMEM((clusters, groups, span, CLASSES), f32),
             pltpu.VMEM((groups, CLASSES, width), bf16),
             pltpu.VMEM((groups, 8, width), f32),
+            pltpu.VMEM((groups // 4, CLASSES + 8, width), f32),
+            pltpu.VMEM((groups // 4, CLASSES + 8, width), f32),
+            pltpu.VMEM((groups // 4, CLASSES + 8, width), f32),
             pltpu.VMEM((groups, CLASSES, width), bf16),
             pltpu.VMEM((groups, 8, width), f32),
             pltpu.VMEM((CLASSES + 8, width), f32),
@@ -445,6 +498,8 @@
             pltpu.SemaphoreType.DMA((groups,)),
             pltpu.SemaphoreType.DMA((groups,)),
             pltpu.SemaphoreType.DMA((groups,)),
+            pltpu.SemaphoreType.DMA((groups // 4,)),
+            pltpu.SemaphoreType.DMA((groups // 4,)),
             pltpu.SemaphoreType.DMA((group,)),
             pltpu.SemaphoreType.DMA((group,)),
         ],

time: 58.8 us -> 56.1 us (0.954)
  Pallas kernels: 57.2 us -> 54.2 us
    pallas_call x1, Pallas kernels: 57.2 us -> 54.2 us  [local(): pl.pallas_call(functools.partial(kernel, cfg), out_shape=jax.ShapeDtypeSt...]
where the time goes in v6:
time: 56.1 us; the launch traced here: 55.6 us
  Pallas kernels  54.2 us (97%)
  other arithmetic  1.38 us (2%)
    pallas_call x1, Pallas kernels, local(): pl.pallas_call(functools.partial(kernel, cfg), out_shape=jax.ShapeDtypeSt...  54.2 us
    mul x1, other arithmetic, local(): pl.pallas_call(functools.partial(kernel, cfg), out_shape=jax.ShapeDtypeSt...  1.38 us

profile of v6, /device:TPU:0, one launch (start us, length us, event | category | flops | bytes accessed | tf_op | source)
XLA Modules:
  0.0 55.6 jit_solution(425057710621484322)
XLA Ops:
  0.0 54.2 %shard_map.46 = f32[64,128]{1,0:T(8,128)} custom-call(bf16[64,768]{1,0:T(8,128)(2,1)} %query_ref.1, s32[8,64]{1,0:T(8,128)} %bitcast.1, s32[8,1024]{1,0:T(8,128)} %labels_ref.1, bf16[8,1024,768]{2,1,0:T(8,128)(2,1)} %bank_ref.1), custom_call_target="tpu_custom_call" | custom-call | tf_op jit(solution)/shard_map/pallas_call | solution.py:470
  54.2 1.4 %broadcast_multiply_fusion = f32[64,128]{1,0:T(8,128)} fusion(f32[64,128]{1,0:T(8,128)} %shard_map.46), kind=kLoop, calls=%fused_computation | loop fusion | flops 8192 | bytes 65536 | tf_op jit(solution)/shard_map/mul | solution.py:470
